TPU v7x, 128 devices: a whole 4x4x4 slice. The times are simulated.
128 devices in a mesh: rows: 64 (over x, z, y), cols: 2 (over core).
Axes of the slice: x: 4, y: 4, z: 4, core: 2. Of those that a mesh axis runs over, the one named last changes fastest.
Arguments:
- blocks: bfloat16 [4096, 7, 128, 128], P('rows'), may hold values from -0.1875 to 0.1875
- col_index: int32 [4096, 7], P('rows'), may hold values from 0 to 4095, as said below
- right_vecs: bfloat16 [64, 4096, 128], P('cols', 'rows'), may hold values from -30 to 30
- left_vecs: bfloat16 [64, 4096, 128], P('cols', 'rows'), may hold values from -30 to 30
- ritz: bfloat16 [64, 64], replicated, may hold values from -0.75 to 0.75
Outputs:
- right_res: float32 [64, 4096, 128], P('cols', 'rows')
- left_res: float32 [64, 4096, 128], P('cols', 'rows')
- right_norms: float32 [64], P('cols')
- left_norms: float32 [64], P('cols')
Inputs may be any that keep to these rules, and one draw needn't show every extreme that they name: `col_index`: entry 0 of each block row is the row's own index. Device p of rows holds block rows p * 64 to (p + 1) * 64 - 1. The devices form a grid of 2 x (32) subdomains of the slab, p = i * M + j with M = 32, periodic along j. Columns outside a device's own rows lie only on its three face neighbours: (i, j + 1 mod M), (i, j - 1 mod M) and (1 - i, j). Among the entries of one device's block rows exactly 2 have a column on (i, j + 1 mod M), and 1 to 2 on each of the other two.
All inputs are finite; a program needn't handle non-finite values.
Results may differ from a plain program's by a relative error of at most 0.0006.
Values may be sent and summed in bfloat16 or wider, within the bound.
A program may use at most 128 MiB of HBM per device.

v0:
```python
import jax
import jax.numpy as jnp
from jax import lax
from jax.sharding import PartitionSpec as P

SENDS = 2


def shards(blocks, col_index, right_vecs, left_vecs, ritz):
    peers = lax.axis_size("rows")
    me = lax.axis_index("rows")
    rows_here = col_index.shape[0]
    slots = col_index.shape[1]
    vec_here = right_vecs.shape[0]
    width = right_vecs.shape[2]
    owner = (col_index // rows_here).reshape(-1)
    local_id = (col_index % rows_here).reshape(-1)
    remote = owner != me
    onehot = (owner[:, None] == jnp.arange(peers, dtype=jnp.int32)[None, :]).astype(jnp.int32)
    rank = jnp.sum(jnp.cumsum(onehot, axis=0) * onehot, axis=1) - 1
    ext_index = jnp.where(remote, rows_here + owner * SENDS + rank, local_id)
    target = jnp.where(remote, owner, peers)
    wanted = jnp.zeros((peers, SENDS), jnp.int32).at[target, rank].set(local_id, mode="drop")
    asked = lax.all_to_all(wanted, "rows", split_axis=0, concat_axis=0, tiled=True)
    asked_flat = asked.reshape(-1)
    outgoing = right_vecs[:, asked_flat, :]
    contrib = jnp.einsum("kra,rsab->krsb", left_vecs, blocks, preferred_element_type=jnp.float32)
    contrib = contrib.reshape(vec_here, rows_here * slots, width)
    summed = (
        jnp.zeros((vec_here, rows_here + peers * SENDS, width), jnp.float32)
        .at[:, ext_index, :]
        .add(contrib)
    )
    incoming = lax.all_to_all(outgoing, "rows", split_axis=1, concat_axis=1, tiled=True)
    returned = lax.all_to_all(
        summed[:, rows_here:, :].astype(jnp.bfloat16),
        "rows",
        split_axis=1,
        concat_axis=1,
        tiled=True,
    ).astype(jnp.float32)
    extended = jnp.concatenate([right_vecs, incoming], axis=1)
    gathered = extended[:, ext_index, :].reshape(vec_here, rows_here, slots, width)
    product = jnp.einsum("krsj,rsij->kri", gathered, blocks, preferred_element_type=jnp.float32)
    transposed = summed[:, :rows_here, :].at[:, asked_flat, :].add(returned)
    mine = lax.axis_index("cols") * vec_here
    full_right, full_left = (
        lax.all_gather(right_vecs, "cols", axis=0, tiled=True),
        lax.all_gather(left_vecs, "cols", axis=0, tiled=True),
    )
    total = ritz.shape[0]
    right_table = lax.dynamic_slice(ritz, (0, mine), (total, vec_here))
    left_table = lax.dynamic_slice(ritz.T, (0, mine), (total, vec_here))
    right_shift = jnp.einsum(
        "krb,kq->qrb", full_right, right_table, preferred_element_type=jnp.float32
    )
    left_shift = jnp.einsum(
        "krb,kq->qrb", full_left, left_table, preferred_element_type=jnp.float32
    )
    right_res = product - right_shift
    left_res = transposed - left_shift
    right_sq, left_sq = lax.psum(
        (jnp.sum(right_res * right_res, axis=(1, 2)), jnp.sum(left_res * left_res, axis=(1, 2))),
        "rows",
    )
    return (right_res, left_res, jnp.sqrt(right_sq), jnp.sqrt(left_sq))


def solution(mesh):
    placed = (
        P("rows", None, None, None),
        P("rows", None),
        P("cols", "rows", None),
        P("cols", "rows", None),
        P(),
    )
    return jax.shard_map(
        shards,
        mesh=mesh,
        in_specs=placed,
        out_specs=(P("cols", "rows", None), P("cols", "rows", None), P("cols"), P("cols")),
        check_vma=False,
    )
```

profile of v0, /device:TPU:0, one launch (start us, length us, event | category | flops | bytes accessed | tf_op | source)
XLA Modules:
  0.0 374.0 jit_solution(11511773437690598463)
XLA Ops:
  8.8 1.2 reduce-window.6
  10.4 21.3 %scatter_fusion = s32[64,2]{0,1:T(2,128)S(1)} fusion(s32[64,2]{0,1:T(2,128)S(1)} %broadcast_in_dim.8, s32[448]{0:T(512)S(1)} %bitcast.54, s32[448]{0:T(512)S(1)} %reshape.185), kind=kCustom, calls=%fused_computation.2 | custom fusion | bytes 8960 | tf_op jit(solution)/shard_map/scatter | solution.py:23
  32.5 11.5 %all-to-all-start = ((s32[64,1,2]{2,1,0:T(1,128)}), s32[64,1,2]{2,1,0:T(1,128)S(1)}, u32[]{:S(2)}, u32[]{:S(2)}) async-start(s32[64,1,2]{2,1,0:T(1,128)} %copy.36), calls=%async_computation | async-start | bytes 65536 | tf_op jit(solution)/shard_map/all_to_all | solution.py:24
  44.0 10.5 %fusion = f32[64,7,128,32]{2,3,1,0:T(8,128)} fusion(bf16[64,7,128,128]{3,2,1,0:T(8,128)(2,1)} %param.5, bf16[32,64,128,1]{2,1,0,3:T(8,128)(2,1)S(1)} %bitcast.57), kind=kOutput, calls=%fused_computation.13 | convolution fusion | flops 469762048 | bytes 22544384 | tf_op jit(solution)/shard_map/kra,rsab->krsb/dot_general | solution.py:27
  54.5 2.1 broadcast_in_dim.10
  56.6 59.6 %scatter_fusion.1 = f32[32,192,128]{2,0,1:T(8,128)} fusion(f32[32,192,128]{2,0,1:T(8,128)} %broadcast_in_dim.10, s32[448]{0:T(512)S(1)} %bitcast.58, f32[448,32,128]{2,1,0:T(8,128)} %bitcast.53), kind=kCustom, calls=%fused_computation.3 | custom fusion | flops 1835008 | bytes 22021888 | tf_op jit(solution)/shard_map/scatter-add | solution.py:32
  116.2 2.8 slice.36
  119.0 10.3 %all-to-all-start.2 = ((bf16[32,128,128]{2,0,1:T(8,128)(2,1)}), bf16[32,128,128]{2,0,1:T(8,128)(2,1)S(1)}, u32[]{:S(2)}, u32[]{:S(2)}) async-start(bf16[32,128,128]{2,0,1:T(8,128)(2,1)} %slice.36), calls=%async_computation.2 | async-start | bytes 2097152 | tf_op jit(solution)/shard_map/all_to_all | solution.py:35
  132.2 5.2 %gather_fusion = bf16[128,32,128]{2,0,1:T(8,128)(2,1)S(1)} fusion(bf16[32,64,128]{2,1,0:T(8,128)(2,1)S(1)} %copy-done.1, s32[1024]{0:T(1024)S(1)} %pad_clamp_fusion.1), kind=kCustom, calls=%fused_computation | custom fusion | bytes 2097664 | tf_op jit(solution)/shard_map/gather | solution.py:26
  137.4 1.6 copy.37
  139.0 8.3 %all-to-all-done.2 = bf16[32,128,128]{2,0,1:T(8,128)(2,1)S(1)} async-done(((bf16[32,128,128]{2,0,1:T(8,128)(2,1)}), bf16[32,128,128]{2,0,1:T(8,128)(2,1)S(1)}, u32[]{:S(2)}, u32[]{:S(2)}) %all-to-all-start.2) | async-done | bytes 1048608 | tf_op jit(solution)/shard_map/all_to_all | solution.py:35
  147.3 5.5 %all-to-all-start.1 = ((bf16[32,128,128]{2,0,1:T(8,128)(2,1)}), bf16[32,128,128]{2,0,1:T(8,128)(2,1)}, u32[]{:S(2)}, u32[]{:S(2)}) async-start(bf16[32,128,128]{2,0,1:T(8,128)(2,1)} %copy.37), calls=%async_computation.1 | async-start | bytes 2097152 | tf_op jit(solution)/shard_map/all_to_all | solution.py:34
  154.1 1.3 slice.29
  155.4 1.5 convert_bitcast_fusion
  156.9 5.9 %scatter_fusion.2 = f32[32,64,128]{2,0,1:T(8,128)S(1)} fusion(f32[32,64,128]{2,0,1:T(8,128)S(1)} %slice.29, s32[128]{0:T(128)S(1)} %fusion.10, f32[128,32,128]{2,1,0:T(8,128)S(1)} %convert_bitcast_fusion), kind=kCustom, calls=%fused_computation.4 | custom fusion | flops 524288 | bytes 6291968 | tf_op jit(solution)/shard_map/scatter-add | solution.py:45
  162.9 6.7 %all-to-all-done.1 = bf16[32,128,128]{2,0,1:T(8,128)(2,1)} async-done(((bf16[32,128,128]{2,0,1:T(8,128)(2,1)}), bf16[32,128,128]{2,0,1:T(8,128)(2,1)}, u32[]{:S(2)}, u32[]{:S(2)}) %all-to-all-start.1) | async-done | bytes 1048608 | tf_op jit(solution)/shard_map/all_to_all | solution.py:34
  169.6 1.5 pad_maximum_fusion
  171.1 3.4 gather_fusion.1
  174.4 11.4 %convolution_bitcast_fusion = f32[32,64,128]{2,0,1:T(8,128)S(1)} fusion(bf16[32,64,7,128]{3,0,2,1:T(8,128)(2,1)} %bitcast.55, bf16[64,7,128,128]{3,2,1,0:T(8,128)(2,1)} %param.5), kind=kOutput, calls=%fused_computation.10 | convolution fusion | flops 469762048 | bytes 19398656 | tf_op jit(solution)/shard_map/krsj,rsij->kri/dot_general | solution.py:44
  185.9 1.6 multiply_reduce_fusion
  187.6 1.7 multiply_reduce_fusion.1
  189.3 173.7 %all-reduce.1 = (f32[32]{0:T(128)S(1)}, f32[32]{0:T(128)S(1)}) all-reduce(f32[32]{0:T(128)S(1)} %get-tuple-element.24, f32[32]{0:T(128)S(1)} %get-tuple-element.26), channel_id=1, replica_groups=mesh['rows'=64,'cols'=2] {'rows'}, use_global_device_ids=true, to_apply=%region_7.8 | all-reduce | flops 64 | bytes 512 | tf_op jit(solution)/shard_map/psum | solution.py:62
  364.0 1.6 copy.45
  365.6 1.6 copy.44
  (43 shorter events, 7.8 us)
Async XLA Ops:
  7.2 178.7 %copy-start = (bf16[64,64]{1,0:T(8,128)(2,1)S(1)}, bf16[64,64]{1,0:T(8,128)(2,1)}, u32[]{:S(2)}) copy-start(bf16[64,64]{1,0:T(8,128)(2,1)} %param.9) | copy-start | bytes 24580
  7.2 36.8 %copy-start.3 = (bf16[32,64,128]{2,1,0:T(8,128)(2,1)S(1)}, bf16[32,64,128]{2,1,0:T(8,128)(2,1)}, u32[]{:S(2)}) copy-start(bf16[32,64,128]{2,1,0:T(8,128)(2,1)} %param.8) | copy-start | bytes 1572868
  32.5 86.6 %all-to-all-start = ((s32[64,1,2]{2,1,0:T(1,128)}), s32[64,1,2]{2,1,0:T(1,128)S(1)}, u32[]{:S(2)}, u32[]{:S(2)}) async-start(s32[64,1,2]{2,1,0:T(1,128)} %copy.36), calls=%async_computation | async-start | bytes 65536 | tf_op jit(solution)/shard_map/all_to_all | solution.py:24
  116.2 16.0 %copy-start.1 = (bf16[32,64,128]{2,1,0:T(8,128)(2,1)S(1)}, bf16[32,64,128]{2,1,0:T(8,128)(2,1)}, u32[]{:S(2)}) copy-start(bf16[32,64,128]{2,1,0:T(8,128)(2,1)} %param.7) | copy-start | bytes 1572868
  119.0 28.3 %all-to-all-start.2 = ((bf16[32,128,128]{2,0,1:T(8,128)(2,1)}), bf16[32,128,128]{2,0,1:T(8,128)(2,1)S(1)}, u32[]{:S(2)}, u32[]{:S(2)}) async-start(bf16[32,128,128]{2,0,1:T(8,128)(2,1)} %slice.36), calls=%async_computation.2 | async-start | bytes 2097152 | tf_op jit(solution)/shard_map/all_to_all | solution.py:35
  129.4 56.5 %all-gather.5.cloned.1.call-start = ((), (), s32[]{:S(2)}) async-start(), calls=%async_computation.4 | async-start | bytes 1572864 | tf_op jit(solution)/shard_map/all_gather | solution.py:49
  147.3 6.7 %copy-start.2 = (bf16[32,128,128]{2,0,1:T(8,128)(2,1)}, bf16[32,128,128]{2,0,1:T(8,128)(2,1)S(1)}, u32[]{:S(2)}) copy-start(bf16[32,128,128]{2,0,1:T(8,128)(2,1)S(1)} %all-to-all-done.2) | copy-start | bytes 3145732
  147.3 22.2 %all-to-all-start.1 = ((bf16[32,128,128]{2,0,1:T(8,128)(2,1)}), bf16[32,128,128]{2,0,1:T(8,128)(2,1)}, u32[]{:S(2)}, u32[]{:S(2)}) async-start(bf16[32,128,128]{2,0,1:T(8,128)(2,1)} %copy.37), calls=%async_computation.1 | async-start | bytes 2097152 | tf_op jit(solution)/shard_map/all_to_all | solution.py:34
  152.9 34.7 %all-gather.3.cloned.1.call-start = ((), (), s32[]{:S(2)}) async-start(), calls=%async_computation.3 | async-start | bytes 1572864 | tf_op jit(solution)/shard_map/all_gather | solution.py:48
Sparse Core Ops, SparseCore 0:
  131.9 12.9 all-gather.4
  155.4 12.9 all-gather.2
where the time goes:
time: 375 us; the launch traced here: 374 us
  blocking collectives  174 us (46%)
  other arithmetic  71.5 us (19%)
  local copies, waits for them, and re-layouts  46.6 us (12%)
  starting transfers between devices  27.6 us (7%)
  matrix products  25.3 us (7%)
  waiting for transfers between devices  15.1 us (4%)
  between operations  14.3 us (4%)
    psum x1, blocking collectives, shards(): lax.psum((jnp.sum(right_res * right_res, axis=(1, 2)), jnp.sum(left_res *...  174 us
    scatter-add x1, other arithmetic, shards(): summed = jnp.zeros((vec_here, rows_here + peers * SENDS, width), jnp.floa...  59.6 us
    scatter x1, local copies, waits for them, and re-layouts, shards(): jnp.zeros((peers, SENDS), jnp.int32).at[target, rank]  21.3 us
    all_to_all x1, starting transfers between devices, shards(): lax.all_to_all(wanted, 'rows', split_axis=0, concat_axis=0, tiled=True)  11.5 us
    dot_general x1, matrix products, shards(): jnp.einsum('krsj,rsij->kri', gathered, blocks, preferred_element_type=jnp...  11.4 us
    dot_general x1, matrix products, shards(): jnp.einsum('kra,rsab->krsb', left_vecs, blocks, preferred_element_type=jn...  10.5 us
    all_to_all x1, starting transfers between devices, shards(): lax.all_to_all(summed[:, rows_here:, :].astype(jnp.bfloat16), 'rows', spl...  10.3 us
    all_to_all x1, waiting for transfers between devices, shards(): lax.all_to_all(summed[:, rows_here:, :].astype(jnp.bfloat16), 'rows', spl...  8.32 us
  transfers between devices with their start and end apart: 5, of which 2 were waited for; matrix products, arithmetic and copies ran while one was open for 30% of the time, Pallas kernels for 0%

commit v1 on v0

--- a/solution.py
+++ b/solution.py
@@ -32,12 +32,18 @@
         .add(contrib)
     )
     incoming = lax.all_to_all(outgoing, "rows", split_axis=1, concat_axis=1, tiled=True)
-    returned = lax.all_to_all(
-        summed[:, rows_here:, :].astype(jnp.bfloat16),
-        "rows",
-        split_axis=1,
-        concat_axis=1,
-        tiled=True,
+    returned = jnp.concatenate(
+        lax.all_to_all(
+            jnp.stack(
+                jnp.split(
+                    summed[:, rows_here:, :].astype(jnp.bfloat16), lax.axis_size("rows"), axis=1
+                )
+            ),
+            "rows",
+            0,
+            0,
+        ),
+        axis=1,
     ).astype(jnp.float32)
     extended = jnp.concatenate([right_vecs, incoming], axis=1)
     gathered = extended[:, ext_index, :].reshape(vec_here, rows_here, slots, width)

time: 375 us -> 392 us (1.045)
  local copies, waits for them, and re-layouts: 46.6 us -> 82.2 us
  other arithmetic: 71.5 us -> 52.2 us
    unnamed x12 -> x79, local copies, waits for them, and re-layouts: 5.47 us -> 45 us
    scatter-add x1, other arithmetic: 59.6 us -> 40 us  [shards(): summed = jnp.zeros((vec_here, rows_here + peers * SENDS, width), jnp.floa...]
  transfers between devices with their start and end apart: 5 -> 5, of which waited for: 2 -> 2; matrix products, arithmetic and copies ran while one was open for 30% -> 33% of each run, Pallas kernels for 0% -> 0%
where the time goes in v1:
time: 392 us; the launch traced here: 390 us
  blocking collectives  174 us (44%)
  local copies, waits for them, and re-layouts  82.2 us (21%)
  other arithmetic  52.2 us (13%)
  starting transfers between devices  27.7 us (7%)
  matrix products  25.3 us (6%)
  waiting for transfers between devices  15 us (4%)
  between operations  14.3 us (4%)
    psum x1, blocking collectives, shards(): lax.psum((jnp.sum(right_res * right_res, axis=(1, 2)), jnp.sum(left_res *...  174 us
    unnamed x79, local copies, waits for them, and re-layouts  45 us
    scatter-add x1, other arithmetic, shards(): summed = jnp.zeros((vec_here, rows_here + peers * SENDS, width), jnp.floa...  40 us
    scatter x1, local copies, waits for them, and re-layouts, shards(): jnp.zeros((peers, SENDS), jnp.int32).at[target, rank]  21.3 us
    all_to_all x1, starting transfers between devices, shards(): lax.all_to_all(wanted, 'rows', split_axis=0, concat_axis=0, tiled=True)  11.5 us
    dot_general x1, matrix products, shards(): jnp.einsum('krsj,rsij->kri', gathered, blocks, preferred_element_type=jnp...  11.4 us
    dot_general x1, matrix products, shards(): jnp.einsum('kra,rsab->krsb', left_vecs, blocks, preferred_element_type=jn...  10.5 us
    all_to_all x1, starting transfers between devices, shards(): lax.all_to_all(jnp.stack(jnp.split(summed[:, rows_here:, :].astype(jnp.bf...  10.4 us
  transfers between devices with their start and end apart: 5, of which 2 were waited for; matrix products, arithmetic and copies ran while one was open for 33% of the time, Pallas kernels for 0%

profile of v1, /device:TPU:0, one launch (start us, length us, event | category | flops | bytes accessed | tf_op | source)
XLA Modules:
  0.0 390.5 jit_solution(649903157686062535)
XLA Ops:
  8.7 1.2 reduce-window.6
  10.4 21.3 %scatter_fusion = s32[64,2]{0,1:T(2,128)S(1)} fusion(s32[64,2]{0,1:T(2,128)S(1)} %broadcast_in_dim.8, s32[448]{0:T(512)S(1)} %bitcast.313, s32[448]{0:T(512)S(1)} %reshape.190), kind=kCustom, calls=%fused_computation.2 | custom fusion | bytes 8960 | tf_op jit(solution)/shard_map/scatter | solution.py:23
  32.4 11.5 %all-to-all-start = ((s32[64,1,2]{2,1,0:T(1,128)}), s32[64,1,2]{2,1,0:T(1,128)S(1)}, u32[]{:S(2)}, u32[]{:S(2)}) async-start(s32[64,1,2]{2,1,0:T(1,128)} %copy.36), calls=%async_computation | async-start | bytes 65536 | tf_op jit(solution)/shard_map/all_to_all | solution.py:24
  43.9 10.5 %fusion = f32[64,7,128,32]{2,3,1,0:T(8,128)} fusion(bf16[64,7,128,128]{3,2,1,0:T(8,128)(2,1)} %param.5, bf16[32,64,128,1]{2,1,0,3:T(8,128)(2,1)S(1)} %bitcast.317), kind=kOutput, calls=%fused_computation.11 | convolution fusion | flops 469762048 | bytes 22544384 | tf_op jit(solution)/shard_map/kra,rsab->krsb/dot_general | solution.py:27
  54.8 40.0 %scatter_fusion.1 = f32[32,192,128]{2,0,1:T(8,128)S(1)} fusion(f32[32,192,128]{2,0,1:T(8,128)S(1)} %broadcast_in_dim.10, s32[448]{0:T(512)S(1)} %bitcast.318, f32[448,32,128]{2,1,0:T(8,128)} %bitcast.312), kind=kCustom, calls=%fused_computation.3 | custom fusion | flops 1835008 | bytes 22021888 | tf_op jit(solution)/shard_map/scatter-add | solution.py:32
  95.2 1.3 copy-done.2
  135.4 10.4 %all-to-all-start.2 = ((bf16[64,32,2,128]{3,1,2,0:T(8,128)(2,1)}), bf16[64,32,2,128]{3,1,2,0:T(8,128)(2,1)S(1)}, u32[]{:S(2)}, u32[]{:S(2)}) async-start(bf16[64,32,2,128]{3,1,2,0:T(8,128)(2,1)} %constant_dynamic-update-slice_fusion), calls=%async_computation.2 | async-start | bytes 2097152 | tf_op jit(solution)/shard_map/all_to_all | solution.py:36
  146.0 1.2 copy.43
  148.6 5.2 %gather_fusion = bf16[128,32,128]{2,0,1:T(8,128)(2,1)S(1)} fusion(bf16[32,64,128]{2,1,0:T(8,128)(2,1)S(1)} %copy-done.1, s32[1024]{0:T(1024)S(1)} %pad_clamp_fusion.1), kind=kCustom, calls=%fused_computation | custom fusion | bytes 2097664 | tf_op jit(solution)/shard_map/gather | solution.py:26
  153.8 1.6 copy.37
  155.5 8.3 %all-to-all-done.2 = bf16[64,32,2,128]{3,1,2,0:T(8,128)(2,1)S(1)} async-done(((bf16[64,32,2,128]{3,1,2,0:T(8,128)(2,1)}), bf16[64,32,2,128]{3,1,2,0:T(8,128)(2,1)S(1)}, u32[]{:S(2)}, u32[]{:S(2)}) %all-to-all-start.2) | async-done | bytes 1048608 | tf_op jit(solution)/shard_map/all_to_all | solution.py:36
  163.8 5.5 %all-to-all-start.1 = ((bf16[32,128,128]{2,0,1:T(8,128)(2,1)}), bf16[32,128,128]{2,0,1:T(8,128)(2,1)}, u32[]{:S(2)}, u32[]{:S(2)}) async-start(bf16[32,128,128]{2,0,1:T(8,128)(2,1)} %copy.37), calls=%async_computation.1 | async-start | bytes 2097152 | tf_op jit(solution)/shard_map/all_to_all | solution.py:34
  170.5 1.3 slice.90
  171.8 1.5 convert_element_type.16
  173.4 5.9 %scatter_fusion.2 = f32[32,64,128]{2,0,1:T(8,128)S(1)} fusion(f32[32,64,128]{2,0,1:T(8,128)S(1)} %slice.90, s32[128]{0:T(128)S(1)} %fusion.10, f32[128,32,128]{2,1,0:T(8,128)S(1)} %bitcast.315), kind=kCustom, calls=%fused_computation.4 | custom fusion | flops 524288 | bytes 6291968 | tf_op jit(solution)/shard_map/scatter-add | solution.py:51
  179.3 6.7 %all-to-all-done.1 = bf16[32,128,128]{2,0,1:T(8,128)(2,1)} async-done(((bf16[32,128,128]{2,0,1:T(8,128)(2,1)}), bf16[32,128,128]{2,0,1:T(8,128)(2,1)}, u32[]{:S(2)}, u32[]{:S(2)}) %all-to-all-start.1) | async-done | bytes 1048608 | tf_op jit(solution)/shard_map/all_to_all | solution.py:34
  186.0 1.5 pad_maximum_fusion
  187.5 3.4 gather_fusion.1
  190.8 11.4 %convolution_bitcast_fusion = f32[32,64,128]{2,0,1:T(8,128)S(1)} fusion(bf16[32,64,7,128]{3,0,2,1:T(8,128)(2,1)} %bitcast.314, bf16[64,7,128,128]{3,2,1,0:T(8,128)(2,1)} %param.5), kind=kOutput, calls=%fused_computation.8 | convolution fusion | flops 469762048 | bytes 19398656 | tf_op jit(solution)/shard_map/krsj,rsij->kri/dot_general | solution.py:50
  202.3 1.6 multiply_reduce_fusion
  204.0 1.7 multiply_reduce_fusion.1
  205.7 173.7 %all-reduce.1 = (f32[32]{0:T(128)S(1)}, f32[32]{0:T(128)S(1)}) all-reduce(f32[32]{0:T(128)S(1)} %get-tuple-element.24, f32[32]{0:T(128)S(1)} %get-tuple-element.26), channel_id=1, replica_groups=mesh['rows'=64,'cols'=2] {'rows'}, use_global_device_ids=true, to_apply=%region_7.8 | all-reduce | flops 64 | bytes 512 | tf_op jit(solution)/shard_map/psum | solution.py:68
  380.5 1.6 copy.45
  382.0 1.6 copy.44
  (111 shorter events, 46.1 us)
Async XLA Ops:
  7.2 195.1 %copy-start = (bf16[64,64]{1,0:T(8,128)(2,1)S(1)}, bf16[64,64]{1,0:T(8,128)(2,1)}, u32[]{:S(2)}) copy-start(bf16[64,64]{1,0:T(8,128)(2,1)} %param.9) | copy-start | bytes 24580
  10.4 33.5 %copy-start.4 = (bf16[32,64,128]{2,1,0:T(8,128)(2,1)S(1)}, bf16[32,64,128]{2,1,0:T(8,128)(2,1)}, u32[]{:S(2)}) copy-start(bf16[32,64,128]{2,1,0:T(8,128)(2,1)} %param.8) | copy-start | bytes 1572868
  32.4 102.9 %all-to-all-start = ((s32[64,1,2]{2,1,0:T(1,128)}), s32[64,1,2]{2,1,0:T(1,128)S(1)}, u32[]{:S(2)}, u32[]{:S(2)}) async-start(s32[64,1,2]{2,1,0:T(1,128)} %copy.36), calls=%async_computation | async-start | bytes 65536 | tf_op jit(solution)/shard_map/all_to_all | solution.py:24
  94.8 1.7 copy-start.2
  115.9 30.1 %copy-start.5 = (bf16[32,64,128]{2,1,0:T(8,128)(2,1)S(1)}, bf16[32,64,128]{2,1,0:T(8,128)(2,1)}, u32[]{:S(2)}) copy-start(bf16[32,64,128]{2,1,0:T(8,128)(2,1)} %param.8) | copy-start | bytes 1572868
  135.3 13.3 %copy-start.1 = (bf16[32,64,128]{2,1,0:T(8,128)(2,1)S(1)}, bf16[32,64,128]{2,1,0:T(8,128)(2,1)}, u32[]{:S(2)}) copy-start(bf16[32,64,128]{2,1,0:T(8,128)(2,1)} %param.7) | copy-start | bytes 1572868
  135.4 28.4 %all-to-all-start.2 = ((bf16[64,32,2,128]{3,1,2,0:T(8,128)(2,1)}), bf16[64,32,2,128]{3,1,2,0:T(8,128)(2,1)S(1)}, u32[]{:S(2)}, u32[]{:S(2)}) async-start(bf16[64,32,2,128]{3,1,2,0:T(8,128)(2,1)} %constant_dynamic-update-slice_fusion), calls=%async_computation.2 | async-start | bytes 2097152 | tf_op jit(solution)/shard_map/all_to_all | solution.py:36
  145.8 56.5 %all-gather.5.cloned.1.call-start = ((), (), s32[]{:S(2)}) async-start(), calls=%async_computation.4 | async-start | bytes 1572864 | tf_op jit(solution)/shard_map/all_gather | solution.py:55
  163.8 6.7 %copy-start.3 = (bf16[64,32,2,128]{3,1,2,0:T(8,128)(2,1)}, bf16[64,32,2,128]{3,1,2,0:T(8,128)(2,1)S(1)}, u32[]{:S(2)}) copy-start(bf16[64,32,2,128]{3,1,2,0:T(8,128)(2,1)S(1)} %all-to-all-done.2) | copy-start | bytes 3145732
  163.8 22.2 %all-to-all-start.1 = ((bf16[32,128,128]{2,0,1:T(8,128)(2,1)}), bf16[32,128,128]{2,0,1:T(8,128)(2,1)}, u32[]{:S(2)}, u32[]{:S(2)}) async-start(bf16[32,128,128]{2,0,1:T(8,128)(2,1)} %copy.37), calls=%async_computation.1 | async-start | bytes 2097152 | tf_op jit(solution)/shard_map/all_to_all | solution.py:34
  169.3 34.7 %all-gather.3.cloned.1.call-start = ((), (), s32[]{:S(2)}) async-start(), calls=%async_computation.3 | async-start | bytes 1572864 | tf_op jit(solution)/shard_map/all_gather | solution.py:54
Sparse Core Ops, SparseCore 0:
  148.3 12.9 all-gather.4
  171.8 12.9 all-gather.2
